TPU v7x, 512 devices: a whole 4x4x16 slice. The times are simulated.
512 devices in a mesh: vocab: 64 (over z, y), tok: 8 (over x, core).
Axes of the slice: x: 4, y: 4, z: 16, core: 2. Of those that a mesh axis runs over, the one named last changes fastest.
Arguments:
- hidden: bfloat16 [1024, 3584], P('tok', 'vocab'), may hold values from -8 to 8
- head_weight: bfloat16 [3584, 81920], P('tok', 'vocab'), may hold values from -4 to 4
- targets: int32 [1024], P('tok'), may hold values from 0 to 81919
- response_mask: int32 [1024], P('tok'), may hold values 0 or 1
- labels: int32 [8], P('tok'), may hold values 0 or 1
- reference_sums: float32 [8, 2], P('tok'), may hold values from -48 to 48
Outputs:
- mean_loss: float32 [], replicated
- margins: float32 [8], P('tok')
- hidden_grad: bfloat16 [1024, 3584], P('tok', 'vocab')
- head_grad: bfloat16 [3584, 81920], P('tok', 'vocab')
All inputs are finite; a program needn't handle non-finite values. No bound on the sum of `response_mask` or of `labels` on one device may be relied on, other than what follows from the above.
Results may differ from a plain program's by a relative error of at most 0.0085.
Values may be sent and summed in bfloat16 or wider, within the bound.
A program may use at most 64 MiB of HBM per device.

v0:
```python
import math
import jax
import jax.numpy as jnp
from jax import lax
from jax.sharding import PartitionSpec as P

beta_scale = 0.1
tie_offset = math.log(2.0)
tie_const = math.log(3.0)
grad_scale = 512.0


def pair_terms(margins, labels):
    winner = labels.astype(jnp.float32)
    log_tie = (
        tie_const
        + margins
        - tie_offset
        - jax.nn.softplus(margins - tie_offset)
        - jax.nn.softplus(margins + tie_offset)
    )
    losses = winner * jax.nn.softplus(tie_offset - margins) - (1.0 - winner) * log_tie
    slopes = -winner * jax.nn.sigmoid(tie_offset - margins) - (1.0 - winner) * (
        1.0 - jax.nn.sigmoid(margins - tie_offset) - jax.nn.sigmoid(margins + tie_offset)
    )
    return (losses, slopes)


def local(hidden, head_weight, targets, response_mask, labels, reference_sums):
    tok_rows = hidden.shape[0]
    vocab_cols = head_weight.shape[1]
    tok_count = lax.axis_size("tok")
    pair_local = labels.shape[0]
    pair_total = pair_local * tok_count
    span = tok_rows // (2 * pair_local)
    rows_full = lax.all_gather(hidden, "vocab", axis=1, tiled=True)
    token_cols = lax.all_to_all(rows_full, "tok", split_axis=1, concat_axis=0, tiled=True)
    head_full = lax.all_gather(head_weight, "tok", axis=0, tiled=True)
    logits = jnp.dot(rows_full, head_full, preferred_element_type=jnp.float32)
    offset = lax.axis_index("vocab") * vocab_cols
    columns = lax.broadcasted_iota(jnp.int32, (1, vocab_cols), 1) + offset
    matched = columns == targets[:, None]
    local_max = jnp.max(logits, axis=1)
    local_target = jnp.sum(jnp.where(matched, logits, 0.0), axis=1)
    row_max = lax.pmax(local_max, "vocab")
    shifted = jnp.exp(logits - row_max[:, None])
    totals, target_logit = lax.psum((jnp.sum(shifted, axis=1), local_target), "vocab")
    probs = shifted / totals[:, None]
    token_logp = target_logit - (row_max + jnp.log(totals))
    weights = response_mask.astype(jnp.float32)
    sequence_logp = jnp.sum((token_logp * weights).reshape(pair_local, 2, span), axis=2)
    ratios = sequence_logp - reference_sums
    margins = beta_scale * (ratios[:, 0] - ratios[:, 1])
    losses, slopes = pair_terms(margins, labels)
    mean_loss = lax.psum(jnp.sum(losses), "tok") / pair_total
    pair_coef = beta_scale * grad_scale / pair_total * slopes
    signed = jnp.stack([pair_coef, -pair_coef], axis=1)
    token_coef = (
        jnp.broadcast_to(signed[:, :, None], (pair_local, 2, span)).reshape(tok_rows) * weights
    )
    onehot = jnp.where(matched, 1.0, 0.0).astype(jnp.float32)
    dlogits = (token_coef[:, None] * (onehot - probs)).astype(jnp.bfloat16)
    dlogit_all = lax.all_gather(dlogits, "tok", axis=0, tiled=True)
    head_grad = lax.dot_general(
        token_cols, dlogit_all, (((0,), (0,)), ((), ())), preferred_element_type=jnp.float32
    ).astype(jnp.bfloat16)
    grad_cols = lax.psum_scatter(
        lax.dot_general(
            head_full, dlogits, (((1,), (1,)), ((), ())), preferred_element_type=jnp.float32
        ),
        "vocab",
        scatter_dimension=0,
        tiled=True,
    )
    hidden_grad = grad_cols.T.astype(jnp.bfloat16)
    return (mean_loss, margins, hidden_grad, head_grad)


def solution(mesh):
    return jax.shard_map(
        local,
        mesh=mesh,
        in_specs=(
            P("tok", "vocab"),
            P("tok", "vocab"),
            P("tok"),
            P("tok"),
            P("tok"),
            P("tok", None),
        ),
        out_specs=(P(), P("tok"), P("tok", "vocab"), P("tok", "vocab")),
        check_vma=False,
    )
```

profile of v0, /device:TPU:6, one launch (start us, length us, event | category | flops | bytes accessed | tf_op | source)
XLA Modules:
  0.0 756.5 jit_solution(17143302099194967058)
XLA Ops:
  7.2 0.0 all-gather.3.cloned.1.call-start
  7.2 0.7 all-gather.3.cloned.1.call-update
  7.9 0.0 all-gather.5.cloned.1.call-start
  8.6 116.4 %all_gather.9 = bf16[128,3584]{0,1:T(8,128)(2,1)} all-gather(bf16[128,56]{0,1:T(8,128)(2,1)} %param.6), channel_id=1, replica_groups=mesh['vocab'=64,'tok'=8] {'vocab'}, dimensions={1}, use_global_device_ids=true | all-gather | bytes 931840 | tf_op jit(solution)/shard_map/all_gather | solution.py:36
  125.0 0.0 copy-start
  125.0 0.0 copy-start.1
  125.0 0.0 copy-start.2
  125.0 0.0 all-gather.3.cloned.1.call-done
  125.0 5.4 fusion.10
  130.4 140.4 %pmax.7 = f32[128]{0:T(128)S(1)} all-reduce(f32[128]{0:T(128)S(1)} %get-tuple-element.22), channel_id=1, replica_groups=mesh['vocab'=64,'tok'=8] {'vocab'}, use_global_device_ids=true, to_apply=%region_3.4 | all-reduce | flops 128 | bytes 1024 | tf_op jit(solution)/shard_map/pmax | solution.py:45
  270.9 0.0 copy-done
  270.9 0.3 fusion.7
  271.2 138.0 %all-reduce.1 = (f32[128]{0:T(128)S(1)}, f32[128]{0:T(128)S(1)}) all-reduce(f32[128]{0:T(128)S(1)} %get-tuple-element.17, f32[128]{0:T(128)S(1)} %get-tuple-element.16), channel_id=1, replica_groups=mesh['vocab'=64,'tok'=8] {'vocab'}, use_global_device_ids=true, to_apply=%region_1.2 | all-reduce | flops 256 | bytes 2048 | tf_op jit(solution)/shard_map/psum | solution.py:47
  409.1 0.0 copy-done.1
  409.2 0.1 reshape.33
  409.2 0.1 reduce_sum.37
  409.4 0.0 copy-done.2
  409.4 0.6 fusion.9
  411.5 0.1 maximum_bitcast_fusion
  411.6 0.1 broadcast_in_dim.26
  411.7 0.1 broadcast_in_dim.27
  411.8 1.0 fusion.6
  412.7 0.0 all-gather.5.cloned.1.call-update
  412.8 4.8 all-to-all-start
  417.6 1.3 dynamic-slice
  419.8 19.0 %psum.23 = f32[]{:T(128)} all-reduce(f32[]{:T(128)} %bitcast.2), channel_id=1, replica_groups=mesh['vocab'=64,'tok'=8] {'tok'}, use_global_device_ids=true, to_apply=%region_7.8 | all-reduce | flops 1 | bytes 8 | tf_op jit(solution)/shard_map/psum | solution.py:55
  438.8 6.9 convolution_bitcast_fusion
  445.7 295.8 %all-reduce.3 = bf16[3584,128]{0,1:T(8,128)(2,1)S(1)} all-reduce(f32[3584,128]{0,1:T(8,128)S(1)} %convolution_bitcast_fusion), channel_id=2, replica_groups=mesh['vocab'=64,'tok'=8] {'vocab'}, use_global_device_ids=true, to_apply=%region_8.9.clone | all-reduce | flops 458752 | bytes 2752512
  741.5 0.1 fusion.8
  741.6 0.7 copy.14
  743.0 0.0 all-to-all-done
  743.0 0.0 all-gather.5.cloned.1.call-done
  743.0 4.4 fusion
  (4 shorter events, 0.0 us)
Async XLA Ops:
  7.2 117.9 %all-gather.3.cloned.1.call-start = ((), (), s32[]{:S(2)}) async-start(), calls=%async_computation.1 | async-start | bytes 10321920 | tf_op jit(solution)/shard_map/all_gather | solution.py:38
  7.9 735.1 %all-gather.5.cloned.1.call-start = ((), (), s32[]{:S(2)}) async-start(), calls=%async_computation.2 | async-start | bytes 2949120 | tf_op jit(solution)/shard_map/all_gather | solution.py:63
  125.0 145.9 %copy-start = (s32[128]{0:T(128)S(1)}, s32[128]{0:T(128)}, u32[]{:S(2)}) copy-start(s32[128]{0:T(128)} %param.8) | copy-start | bytes 1540
  125.0 284.1 %copy-start.1 = (s32[128]{0:T(128)S(1)}, s32[128]{0:T(128)}, u32[]{:S(2)}) copy-start(s32[128]{0:T(128)} %param.9) | copy-start | bytes 1540
  125.0 284.4 %copy-start.2 = (f32[1,2]{1,0:T(1,128)S(1)}, f32[1,2]{1,0:T(1,128)}, u32[]{:S(2)}) copy-start(f32[1,2]{1,0:T(1,128)} %param.11) | copy-start | bytes 28
  412.8 330.2 %all-to-all-start = ((bf16[128,8,448]{0,2,1:T(8,128)(2,1)}), bf16[128,8,448]{0,2,1:T(8,128)(2,1)}, u32[]{:S(2)}, u32[]{:S(2)}) async-start(bf16[128,8,448]{0,2,1:T(8,128)(2,1)} %bitcast.8), calls=%async_computation | async-start | bytes 1835008 | tf_op jit(solution)/shard_map/all_to_all | solution.py:37
Sparse Core Ops, SparseCore 0:
  10.1 63.2 all-gather.2
  412.9 30.2 all-gather.4
where the time goes:
time: 757 us; the launch traced here: 756 us
  blocking collectives  710 us (94%)
  between operations  20.2 us (3%)
  matrix products  16.6 us (2%)
    unnamed x1, blocking collectives  296 us
    pmax x1, blocking collectives, local(): row_max = lax.pmax(local_max, 'vocab')  140 us
    psum x1, blocking collectives, local(): lax.psum((jnp.sum(shifted, axis=1), local_target), 'vocab')  138 us
    all_gather x1, blocking collectives, local(): rows_full = lax.all_gather(hidden, 'vocab', axis=1, tiled=True)  116 us
    psum x1, blocking collectives, local(): mean_loss = lax.psum(jnp.sum(losses), 'tok') / pair_total  19 us
  transfers between devices with their start and end apart: 3, of which 0 were waited for; matrix products, arithmetic and copies ran while one was open for 1% of the time, Pallas kernels for 0%

commit v1 on v0

--- a/solution.py
+++ b/solution.py
@@ -33,7 +33,9 @@
     pair_local = labels.shape[0]
     pair_total = pair_local * tok_count
     span = tok_rows // (2 * pair_local)
-    rows_full = lax.all_gather(hidden, "vocab", axis=1, tiled=True)
+    rows_full = jnp.concatenate(
+        lax.all_to_all(jnp.stack([hidden] * lax.axis_size("vocab")), "vocab", 0, 0), axis=1
+    )
     token_cols = lax.all_to_all(rows_full, "tok", split_axis=1, concat_axis=0, tiled=True)
     head_full = lax.all_gather(head_weight, "tok", axis=0, tiled=True)
     logits = jnp.dot(rows_full, head_full, preferred_element_type=jnp.float32)

time: 757 us -> 714 us (0.943)
  blocking collectives: 710 us -> 596 us
  waiting for transfers between devices: 0.74 us -> 49.6 us
  starting transfers between devices: 4.91 us -> 25 us
    all_gather x1 -> x0, blocking collectives: 116 us -> none  [local(): rows_full = lax.all_gather(hidden, 'vocab', axis=1, tiled=True)]
    all_to_all x0 -> x1, waiting for transfers between devices: none -> 48.8 us  [local(): lax.all_to_all(jnp.stack([hidden] * lax.axis_size('vocab')), 'vocab', 0, 0)]
    all_to_all x0 -> x1, starting transfers between devices: none -> 19 us  [local(): lax.all_to_all(jnp.stack([hidden] * lax.axis_size('vocab')), 'vocab', 0, 0)]
  transfers between devices with their start and end apart: 3 -> 4, of which waited for: 0 -> 1; matrix products, arithmetic and copies ran while one was open for 1% -> 1% of each run, Pallas kernels for 0% -> 0%
where the time goes in v1:
time: 714 us; the launch traced here: 713 us
  blocking collectives  596 us (83%)
  waiting for transfers between devices  49.6 us (7%)
  starting transfers between devices  25 us (4%)
  between operations  20.2 us (3%)
  matrix products  16.6 us (2%)
    unnamed x1, blocking collectives  295 us
    pmax x1, blocking collectives, local(): row_max = lax.pmax(local_max, 'vocab')  140 us
    psum x1, blocking collectives, local(): lax.psum((jnp.sum(shifted, axis=1), local_target), 'vocab')  138 us
    all_to_all x1, waiting for transfers between devices, local(): lax.all_to_all(jnp.stack([hidden] * lax.axis_size('vocab')), 'vocab', 0, 0)  48.8 us
    psum x1, blocking collectives, local(): mean_loss = lax.psum(jnp.sum(losses), 'tok') / pair_total  22.9 us
    all_to_all x1, starting transfers between devices, local(): lax.all_to_all(jnp.stack([hidden] * lax.axis_size('vocab')), 'vocab', 0, 0)  19 us
  transfers between devices with their start and end apart: 4, of which 1 were waited for; matrix products, arithmetic and copies ran while one was open for 1% of the time, Pallas kernels for 0%

profile of v1, /device:TPU:6, one launch (start us, length us, event | category | flops | bytes accessed | tf_op | source)
XLA Modules:
  0.0 713.4 jit_solution(2390890864857348737)
XLA Ops:
  7.2 0.0 all-gather.3.cloned.1.call-start
  7.2 0.7 all-gather.3.cloned.1.call-update
  7.9 1.8 stack.8
  9.7 19.0 %all-to-all-start = ((bf16[64,128,56]{1,2,0:T(8,128)(2,1)}), bf16[64,128,56]{1,2,0:T(8,128)(2,1)}, u32[]{:S(2)}, u32[]{:S(2)}) async-start(bf16[64,128,56]{1,2,0:T(8,128)(2,1)} %stack.8), calls=%async_computation | async-start | bytes 1835008 | tf_op jit(solution)/shard_map/all_to_all | solution.py:37
  28.6 0.0 all-gather.5.cloned.1.call-start
  29.3 48.8 %all-to-all-done = bf16[64,128,56]{1,2,0:T(8,128)(2,1)} async-done(((bf16[64,128,56]{1,2,0:T(8,128)(2,1)}), bf16[64,128,56]{1,2,0:T(8,128)(2,1)}, u32[]{:S(2)}, u32[]{:S(2)}) %all-to-all-start) | async-done | bytes 917536 | tf_op jit(solution)/shard_map/all_to_all | solution.py:37
  78.2 0.0 all-gather.3.cloned.1.call-done
  78.2 0.0 copy-start
  78.2 0.0 copy-start.1
  78.2 0.0 copy-start.2
  78.2 5.4 fusion.10
  83.6 139.6 %pmax.7 = f32[128]{0:T(128)S(1)} all-reduce(f32[128]{0:T(128)S(1)} %get-tuple-element.22), channel_id=1, replica_groups=mesh['vocab'=64,'tok'=8] {'vocab'}, use_global_device_ids=true, to_apply=%region_3.4 | all-reduce | flops 128 | bytes 1024 | tf_op jit(solution)/shard_map/pmax | solution.py:47
  223.2 0.0 copy-done
  223.2 0.3 fusion.7
  223.5 138.4 %all-reduce.1 = (f32[128]{0:T(128)S(1)}, f32[128]{0:T(128)S(1)}) all-reduce(f32[128]{0:T(128)S(1)} %get-tuple-element.17, f32[128]{0:T(128)S(1)} %get-tuple-element.16), channel_id=1, replica_groups=mesh['vocab'=64,'tok'=8] {'vocab'}, use_global_device_ids=true, to_apply=%region_1.2 | all-reduce | flops 256 | bytes 2048 | tf_op jit(solution)/shard_map/psum | solution.py:49
  361.9 0.0 copy-done.1
  361.9 0.1 reshape.44
  362.0 0.1 reduce_sum.37
  362.1 0.0 copy-done.2
  362.1 0.6 fusion.9
  364.2 0.1 maximum_bitcast_fusion
  364.3 0.1 broadcast_in_dim.26
  364.4 0.1 broadcast_in_dim.27
  364.5 1.0 fusion.6
  365.5 0.0 all-gather.5.cloned.1.call-update
  365.5 1.3 dynamic-slice
  367.4 5.9 all-to-all-start.1
  373.6 22.9 %psum.23 = f32[]{:T(128)} all-reduce(f32[]{:T(128)} %bitcast.4), channel_id=1, replica_groups=mesh['vocab'=64,'tok'=8] {'tok'}, use_global_device_ids=true, to_apply=%region_7.8 | all-reduce | flops 1 | bytes 8 | tf_op jit(solution)/shard_map/psum | solution.py:57
  396.5 6.8 convolution_bitcast_fusion
  403.3 295.1 %all-reduce.3 = bf16[3584,128]{0,1:T(8,128)(2,1)S(1)} all-reduce(f32[3584,128]{0,1:T(8,128)S(1)} %convolution_bitcast_fusion), channel_id=2, replica_groups=mesh['vocab'=64,'tok'=8] {'vocab'}, use_global_device_ids=true, to_apply=%region_8.9.clone | all-reduce | flops 458752 | bytes 2752512
  698.4 0.1 fusion.8
  698.5 0.7 copy.15
  699.9 0.0 all-to-all-done.1
  699.9 0.0 all-gather.5.cloned.1.call-done
  699.9 4.4 fusion
  (4 shorter events, 0.0 us)
Async XLA Ops:
  7.2 71.0 %all-gather.3.cloned.1.call-start = ((), (), s32[]{:S(2)}) async-start(), calls=%async_computation.2 | async-start | bytes 10321920 | tf_op jit(solution)/shard_map/all_gather | solution.py:40
  9.7 68.5 %all-to-all-start = ((bf16[64,128,56]{1,2,0:T(8,128)(2,1)}), bf16[64,128,56]{1,2,0:T(8,128)(2,1)}, u32[]{:S(2)}, u32[]{:S(2)}) async-start(bf16[64,128,56]{1,2,0:T(8,128)(2,1)} %stack.8), calls=%async_computation | async-start | bytes 1835008 | tf_op jit(solution)/shard_map/all_to_all | solution.py:37
  28.6 671.3 %all-gather.5.cloned.1.call-start = ((), (), s32[]{:S(2)}) async-start(), calls=%async_computation.3 | async-start | bytes 2949120 | tf_op jit(solution)/shard_map/all_gather | solution.py:65
  78.2 145.0 %copy-start = (s32[128]{0:T(128)S(1)}, s32[128]{0:T(128)}, u32[]{:S(2)}) copy-start(s32[128]{0:T(128)} %param.8) | copy-start | bytes 1540
  78.2 283.7 %copy-start.1 = (s32[128]{0:T(128)S(1)}, s32[128]{0:T(128)}, u32[]{:S(2)}) copy-start(s32[128]{0:T(128)} %param.9) | copy-start | bytes 1540
  78.2 283.9 %copy-start.2 = (f32[1,2]{1,0:T(1,128)S(1)}, f32[1,2]{1,0:T(1,128)}, u32[]{:S(2)}) copy-start(f32[1,2]{1,0:T(1,128)} %param.11) | copy-start | bytes 28
  367.4 332.5 %all-to-all-start.1 = ((bf16[128,8,448]{0,2,1:T(8,128)(2,1)}), bf16[128,8,448]{0,2,1:T(8,128)(2,1)}, u32[]{:S(2)}, u32[]{:S(2)}) async-start(bf16[128,8,448]{0,2,1:T(8,128)(2,1)} %bitcast.10), calls=%async_computation.1 | async-start | bytes 1835008 | tf_op jit(solution)/shard_map/all_to_all | solution.py:39
Sparse Core Ops, SparseCore 0:
  10.1 63.2 all-gather.2
  365.6 33.0 all-gather.4
